TPU v7x, 1024 devices: a whole 4x8x16 slice. The times are simulated.
1024 devices in a mesh: row: 32 (over z, y_hi), col: 32 (over y_lo, x, core).
Axes of the slice: x: 4, y: 8 (y_hi: 2, y_lo: 4; y = y_hi * 4 + y_lo), z: 16, core: 2. Of those that a mesh axis runs over, the one named last changes fastest.
Arguments:
- pmi: bfloat16 [32768, 32768], P('col', 'row'), may hold values from -0.03125 to 0.03125
- tile_mask: int32 [256, 256], P('col', 'row'), may hold values 0 or 1
- probe: bfloat16 [32768, 256], P('row', 'col'), may hold values from -6 to 6
Outputs:
- basis: float32 [32768, 256], P(('row', 'col'))
- factor: float32 [256, 256], replicated
All inputs are finite; a program needn't handle non-finite values. No bound on the sum of `tile_mask` on one device may be relied on, other than what follows from the above.
Results may differ from a plain program's by a relative error of at most 0.0021.
Values may be sent and summed in bfloat16 or wider, within the bound.
No kernel may reach another device: no remote copies, remote signals or barrier semaphores. Data moves between devices by JAX's collectives and lax.ppermute only.
A program may use at most 32 MiB of HBM per device.

v0:
```python
import functools
import math

import jax
import jax.numpy as jnp
from jax import lax
from jax.experimental import pallas as pl
from jax.experimental.pallas import tpu as pltpu
from jax.sharding import Mesh
from jax.sharding import PartitionSpec as P

TILE = 128


Z, Y, CHIP, CORE = "z", "y_hi", ("y_lo", "x"), "core"
ROW, COL, PLANE = (Z, Y), CHIP + (CORE,), (Y,) + CHIP
LIMIT = 32767.0


def exchange(blocks, axis):
    return lax.all_to_all(blocks, axis, split_axis=0, concat_axis=0, tiled=True)


def spread(block, axis):
    n = lax.axis_size(axis)
    return exchange(jnp.broadcast_to(block[None], (n,) + block.shape), axis)


def swap(block, axis):
    return lax.ppermute(block, axis, [(0, 1), (1, 0)])


def scatter_sum(whole, axis):
    n = lax.axis_size(axis)
    rows, columns = whole.shape
    return jnp.sum(exchange(whole.reshape(n, rows // n, columns), axis), axis=0)


def scatter_sum_16(pieces, axis):
    n, _, columns = pieces.shape
    top = jnp.max(jnp.abs(pieces), axis=1, keepdims=True)
    power = jnp.ceil(jnp.log2(jnp.maximum(top, 1e-30)) + 0.001)
    coded = jnp.round(pieces * (jnp.exp2(-power) * LIMIT)).astype(jnp.int16)
    powers = jnp.broadcast_to(power.astype(jnp.int16), (n, 8, columns))
    came = exchange(jnp.concatenate([coded, powers], axis=1), axis)
    unit = jnp.exp2(came[:, -1:].astype(jnp.float32)) * (1 / LIMIT)
    return jnp.sum(came[:, :-8].astype(jnp.float32) * unit, axis=0)


def chip_scatter_sum(whole):
    n = lax.axis_size(CHIP)
    rows, columns = whole.shape
    halves = whole.reshape(n, 2, rows // (2 * n), columns)
    core = lax.axis_index(CORE)
    mine = lax.dynamic_index_in_dim(halves, core, axis=1, keepdims=False)
    other = lax.dynamic_index_in_dim(halves, 1 - core, axis=1, keepdims=False)
    return scatter_sum_16(mine + swap(other, CORE), CHIP)


def chip_spread(block):
    mine = spread(block, CHIP)
    other = swap(mine, CORE)
    first = lax.axis_index(CORE) == 0
    both = jnp.stack([jnp.where(first, mine, other), jnp.where(first, other, mine)], axis=1)
    return both.reshape((-1,) + block.shape)


SUB = 8
LANES = 128
PANEL = 64


def eliminate(panel, first):
    height, width = panel.shape
    tiles = height // SUB
    rows = [panel[SUB * v : SUB * (v + 1)] for v in range(tiles)]
    sub = lax.broadcasted_iota(jnp.int32, (SUB, LANES), 0)

    def wide(a):
        return jnp.concatenate([a] * (width // LANES), axis=1)

    done = []
    for t in range(tiles):
        at = first + t * SUB
        pivots = jnp.zeros((SUB, LANES), jnp.float32)
        columns = {
            v: [jnp.broadcast_to(rows[v][:, at + k : at + k + 1], (SUB, LANES)) for k in range(SUB)]
            for v in range(t, tiles)
        }
        for k in range(SUB):
            pivot = jnp.broadcast_to(columns[t][k][k : k + 1], (SUB, LANES))
            inverse = 1.0 / pivot
            pivots = jnp.where(sub == k, pivot, pivots)
            row = jnp.broadcast_to(rows[t][k : k + 1], (SUB, width))
            heads = [jnp.broadcast_to(columns[t][l][k : k + 1], (SUB, LANES)) for l in range(k + 1, SUB)]
            for v in range(t, tiles):
                times = columns[v][k] * inverse
                if v == t:
                    times = jnp.where(sub > k, times, 0.0)
                rows[v] = rows[v] - wide(times) * row
                for l in range(k + 1, SUB):
                    columns[v][l] = columns[v][l] - times * heads[l - k - 1]
        done.append(rows[t] * wide(lax.rsqrt(pivots)))
    return jnp.concatenate(done, axis=0)


def cholesky_qr_kernel(scale, gram_ref, right_ref, factor_ref, basis_ref, work):
    n, size = right_ref.shape
    work[:, :size] = gram_ref[...]
    right = right_ref[...]
    if n < LANES:
        right = jnp.concatenate([right, jnp.zeros((LANES - n, size), jnp.float32)], axis=0)
    work[:, size:] = right.T
    for low in range(0, size, PANEL):
        high = low + PANEL
        panel = eliminate(work[low:high, :], low)
        work[low:high, :] = panel
        if high < size:
            base = high // LANES * LANES
            change = lax.dot_general(
                panel[:, base:size],
                panel,
                (((0,), (0,)), ((), ())),
                precision=lax.Precision.HIGHEST,
                preferred_element_type=jnp.float32,
            )
            work[high:, :] = work[high:, :] - change[high - base :]
    at_row = lax.broadcasted_iota(jnp.int32, (size, size), 0)
    at_column = lax.broadcasted_iota(jnp.int32, (size, size), 1)
    factor_ref[...] = jnp.where(at_row <= at_column, work[:, :size], 0.0)
    basis_ref[...] = work[:, size:].T[:n] * scale


def cholesky_qr(gram, right, scale):
    vmem = pl.BlockSpec(memory_space=pltpu.VMEM)
    size = gram.shape[0]
    return pl.pallas_call(
        functools.partial(cholesky_qr_kernel, scale),
        out_shape=(
            jax.ShapeDtypeStruct((size, size), jnp.float32),
            jax.ShapeDtypeStruct(right.shape, jnp.float32),
        ),
        in_specs=[vmem, vmem],
        out_specs=(vmem, vmem),
        scratch_shapes=[pltpu.VMEM((size, size + LANES), jnp.float32)],
        name="cholesky_qr",
    )(gram, right)


def masked(pmi, tile_mask):
    rows, cols = pmi.shape
    scaled = tile_mask.astype(jnp.bfloat16)[:, None, :, None]
    return (pmi.reshape(rows // TILE, TILE, cols // TILE, TILE) * scaled).reshape(rows, cols)


def local(pmi, tile_mask, probe):
    rows, cols = pmi.shape
    again, mask_again = lax.optimization_barrier((pmi, tile_mask))
    probe_full = chip_spread(probe.T).reshape(-1, cols)
    k = probe_full.shape[0]
    partial_value = lax.dot_general(
        masked(pmi, tile_mask), probe_full, (((1,), (1,)), ((), ())), preferred_element_type=jnp.float32
    )
    sketch_rows = scatter_sum_16(partial_value.reshape(lax.axis_size(Z), -1, k), Z)
    sketch_rows = (sketch_rows + swap(sketch_rows, Y)).astype(jnp.bfloat16)
    sketch = spread(sketch_rows, Z).reshape(rows, k)
    image = lax.dot_general(
        masked(again, mask_again), sketch, (((0,), (0,)), ((), ())), preferred_element_type=jnp.float32
    )
    mine = chip_scatter_sum(image)
    gram_part = jnp.dot(
        mine.T, mine, precision=lax.Precision.HIGHEST, preferred_element_type=jnp.float32
    )
    gram_rows = jnp.sum(spread(scatter_sum(gram_part, PLANE), (Z, CORE)), axis=0)
    gram = spread(gram_rows, PLANE).reshape(k, k)
    scale = math.sqrt(cols * lax.axis_size(ROW))
    factor, basis = cholesky_qr(gram, mine, scale)
    return (basis, factor)


def solution(mesh):
    sizes = (mesh.shape["row"] // 2, 2, 4, mesh.shape["col"] // 8, 2)
    parts = Mesh(mesh.devices.reshape(sizes), ROW + COL)
    in_specs = (P(COL, ROW), P(COL, ROW), P(ROW, COL))
    out_specs = (P(ROW + COL, None), P())
    return jax.shard_map(local, mesh=parts, in_specs=in_specs, out_specs=out_specs, check_vma=False)
```

profile of v0, /device:TPU:1, one launch (start us, length us, event | category | flops | bytes accessed | tf_op | source)
XLA Modules:
  0.0 215.4 jit_solution(16236685391811603778)
XLA Ops:
  0.6 0.0 copy-start
  0.6 1.6 broadcast_in_dim.12
  2.2 8.0 %all-to-all-start = ((bf16[16,8,1024]{2,1,0:T(8,128)(2,1)}), bf16[16,8,1024]{2,1,0:T(8,128)(2,1)S(1)}, u32[]{:S(2)}, u32[]{:S(2)}) async-start(bf16[16,8,1024]{2,1,0:T(8,128)(2,1)} %broadcast_in_dim.12), calls=%async_computation | async-start | bytes 524288 | tf_op jit(solution)/shard_map/all_to_all | solution.py:21
  10.2 0.7 convert_element_type.44
  10.9 8.1 %all-to-all-done = bf16[16,8,1024]{2,1,0:T(8,128)(2,1)S(1)} async-done(((bf16[16,8,1024]{2,1,0:T(8,128)(2,1)}), bf16[16,8,1024]{2,1,0:T(8,128)(2,1)S(1)}, u32[]{:S(2)}, u32[]{:S(2)}) %all-to-all-start) | async-done | bytes 262176 | tf_op jit(solution)/shard_map/all_to_all | solution.py:21
  19.1 12.7 %collective-permute-start = (bf16[16,8,1024]{2,1,0:T(8,128)(2,1)S(1)}, bf16[16,8,1024]{2,1,0:T(8,128)(2,1)S(1)}, u32[]{:S(2)}, u32[]{:S(2)}) collective-permute-start(bf16[16,8,1024]{2,1,0:T(8,128)(2,1)S(1)} %all-to-all-done), channel_id=1, source_target_pairs={{0,1},{1,0},{2,3},{3,2},{4,5},{5,4},{6,7},{7,6},{8,9},{9,8},{10,11... | collective-permute-start | bytes 786440 | tf_op jit(solution)/shard_map/ppermute | solution.py:30
  31.8 0.3 mul.83
  32.1 0.0 copy-done
  32.1 0.3 bitcast_multiply_fusion
  32.4 0.5 collective-permute-done
  33.0 0.1 pad_maximum_fusion
  33.0 0.8 abs_reduce_fusion
  33.8 0.2 round-nearest-even_convert_fusion
  34.0 0.0 copy-start.3
  34.1 44.0 %all_to_all.35 = s16[16,72,256]{2,1,0:T(8,128)(2,1)S(1)} all-to-all(s16[16,72,256]{2,1,0:T(8,128)(2,1)S(1)} %pad_add_fusion), channel_id=1, replica_groups=mesh['z'=16,'y_hi'=2,'y_lo'=4,'x'=4,'core'=2] {'z'}, dimensions={0} | all-to-all | bytes 1179648 | tf_op jit(solution)/shard_map/all_to_all | solution.py:21
  78.1 0.2 multiply_reduce_fusion
  78.3 4.7 %collective-permute-start.1 = (f32[64,256]{1,0:T(8,128)S(1)}, f32[64,256]{1,0:T(8,128)S(1)}, u32[]{:S(2)}, u32[]{:S(2)}) collective-permute-start(f32[64,256]{1,0:T(8,128)S(1)} %multiply_reduce_fusion), channel_id=1, source_target_pairs={{0,32},{32,0},{1,33},{33,1},{2,34},{34,2},{3,35},{35,3},{4,36},{36... | collective-permute-start | bytes 196616 | tf_op jit(solution)/shard_map/ppermute | solution.py:30
  83.0 4.2 %collective-permute-done.1 = f32[64,256]{1,0:T(8,128)S(1)} collective-permute-done((f32[64,256]{1,0:T(8,128)S(1)}, f32[64,256]{1,0:T(8,128)S(1)}, u32[]{:S(2)}, u32[]{:S(2)}) %collective-permute-start.1) | collective-permute-done | bytes 65568 | tf_op jit(solution)/shard_map/ppermute | solution.py:30
  87.2 0.9 broadcast_in_dim.14
  88.1 4.6 %all-to-all-start.2 = ((bf16[16,64,256]{2,1,0:T(8,128)(2,1)}), bf16[16,64,256]{2,1,0:T(8,128)(2,1)}, u32[]{:S(2)}, u32[]{:S(2)}) async-start(bf16[16,64,256]{2,1,0:T(8,128)(2,1)} %broadcast_in_dim.14), calls=%async_computation.2 | async-start | bytes 1048576 | tf_op jit(solution)/shard_map/all_to_all | solution.py:21
  92.7 0.0 copy-done.3
  92.7 0.1 copy.23
  92.8 2.6 %copy.24 = bf16[1024,1024]{0,1:T(8,128)(2,1)} copy(bf16[1024,1024]{1,0:T(8,128)(2,1)S(1)} %copy-done) | data formatting | bytes 4194304 | tf_op jit(solution)/shard_map/optimization_barrier | solution.py:158
  95.4 0.0 copy-start.1
  95.4 0.3 mul.80
  95.7 1.2 copy-done.1
  97.0 0.3 bitcast_multiply_fusion.1
  97.3 17.1 %all-to-all-done.2 = bf16[16,64,256]{2,1,0:T(8,128)(2,1)} async-done(((bf16[16,64,256]{2,1,0:T(8,128)(2,1)}), bf16[16,64,256]{2,1,0:T(8,128)(2,1)}, u32[]{:S(2)}, u32[]{:S(2)}) %all-to-all-start.2) | async-done | bytes 524320 | tf_op jit(solution)/shard_map/all_to_all | solution.py:21
  114.4 1.8 fusion.5
  116.2 9.2 %collective-permute-start.2 = (f32[16,32,256]{2,1,0:T(8,128)S(1)}, f32[16,32,256]{2,1,0:T(8,128)S(1)}, u32[]{:S(2)}, u32[]{:S(2)}) collective-permute-start(f32[16,32,256]{2,1,0:T(8,128)S(1)} %dynamic-slice_bitcast_fusion), channel_id=1, source_target_pairs={{0,1},{1,0},{2,3},{3,2},{4,5},{5,4},{6,7},{7,6},{8,9},{9,8},{10,11... | collective-permute-start | bytes 1572872 | tf_op jit(solution)/shard_map/ppermute | solution.py:30
  125.5 1.5 collective-permute-done.2
  127.0 0.1 abs_reduce_fusion.1
  127.1 0.1 round-nearest-even_convert_fusion.1
  127.3 14.2 %all_to_all.36 = s16[16,40,256]{2,1,0:T(8,128)(2,1)S(1)} all-to-all(s16[16,40,256]{2,1,0:T(8,128)(2,1)S(1)} %pad_add_fusion.1), channel_id=1, replica_groups=mesh['z'=16,'y_hi'=2,'y_lo'=4,'x'=4,'core'=2] {'y_lo','x'}, dimensions={0} | all-to-all | bytes 655360 | tf_op jit(solution)/shard_map/all_to_all | solution.py:21
  141.5 0.1 multiply_reduce_fusion.1.right_ref
  141.7 0.0 copy-start.2
  141.7 0.1 copy.28
  141.8 0.3 fusion
  142.1 15.5 %all_to_all.37 = f32[32,8,256]{2,1,0:T(8,128)S(1)} all-to-all(f32[32,8,256]{2,1,0:T(8,128)S(1)} %fusion), channel_id=1, replica_groups=mesh['z'=16,'y_hi'=2,'y_lo'=4,'x'=4,'core'=2] {'y_hi','y_lo','x'}, dimensions={0} | all-to-all | bytes 524288 | tf_op jit(solution)/shard_map/all_to_all | solution.py:21
  157.7 32.7 %all_to_all.38 = f32[32,8,256]{2,1,0:T(8,128)S(1)} all-to-all(f32[32,8,256]{2,1,0:T(8,128)S(1)} %broadcast_in_dim.16), channel_id=1, replica_groups=mesh['z'=16,'y_hi'=2,'y_lo'=4,'x'=4,'core'=2] {'z','core'}, dimensions={0} | all-to-all | bytes 524288 | tf_op jit(solution)/shard_map/all_to_all | solution.py:21
  190.4 14.9 %all_to_all.39 = f32[32,8,256]{2,1,0:T(8,128)} all-to-all(f32[32,8,256]{2,1,0:T(8,128)S(1)} %broadcast_in_dim.17), channel_id=1, replica_groups=mesh['z'=16,'y_hi'=2,'y_lo'=4,'x'=4,'core'=2] {'y_hi','y_lo','x'}, dimensions={0} | all-to-all | bytes 524288 | tf_op jit(solution)/shard_map/all_to_all | solution.py:21
  205.3 0.0 copy-done.2
  205.3 10.0 %cholesky_qr.1 = (f32[256,256]{1,0:T(8,128)}, f32[32,256]{1,0:T(8,128)}) custom-call(f32[256,256]{1,0:T(8,128)} %bitcast.57, f32[32,256]{1,0:T(8,128)} %copy-done.2), custom_call_target="tpu_custom_call" | custom-call | tf_op jit(solution)/shard_map/cholesky_qr/pallas_call | solution.py:137
  (18 shorter events, 0.4 us)
Async XLA Ops:
  0.6 31.5 %copy-start = (bf16[1024,1024]{1,0:T(8,128)(2,1)S(1)}, bf16[1024,1024]{1,0:T(8,128)(2,1)}, u32[]{:S(2)}) copy-start(bf16[1024,1024]{1,0:T(8,128)(2,1)} %param.3) | copy-start | bytes 6291460
  2.2 16.8 %all-to-all-start = ((bf16[16,8,1024]{2,1,0:T(8,128)(2,1)}), bf16[16,8,1024]{2,1,0:T(8,128)(2,1)S(1)}, u32[]{:S(2)}, u32[]{:S(2)}) async-start(bf16[16,8,1024]{2,1,0:T(8,128)(2,1)} %broadcast_in_dim.12), calls=%async_computation | async-start | bytes 524288 | tf_op jit(solution)/shard_map/all_to_all | solution.py:21
  19.1 13.9 %collective-permute-start = (bf16[16,8,1024]{2,1,0:T(8,128)(2,1)S(1)}, bf16[16,8,1024]{2,1,0:T(8,128)(2,1)S(1)}, u32[]{:S(2)}, u32[]{:S(2)}) collective-permute-start(bf16[16,8,1024]{2,1,0:T(8,128)(2,1)S(1)} %all-to-all-done), channel_id=1, source_target_pairs={{0,1},{1,0},{2,3},{3,2},{4,5},{5,4},{6,7},{7,6},{8,9},{9,8},{10,11... | collective-permute-start | bytes 786440 | tf_op jit(solution)/shard_map/ppermute | solution.py:30
  34.0 58.7 %copy-start.3 = (s32[8,8]{1,0:T(8,128)S(1)}, s32[8,8]{1,0:T(8,128)}, u32[]{:S(2)}) copy-start(s32[8,8]{1,0:T(8,128)} %param.4) | copy-start | bytes 772
  78.3 8.9 %collective-permute-start.1 = (f32[64,256]{1,0:T(8,128)S(1)}, f32[64,256]{1,0:T(8,128)S(1)}, u32[]{:S(2)}, u32[]{:S(2)}) collective-permute-start(f32[64,256]{1,0:T(8,128)S(1)} %multiply_reduce_fusion), channel_id=1, source_target_pairs={{0,32},{32,0},{1,33},{33,1},{2,34},{34,2},{3,35},{35,3},{4,36},{36... | collective-permute-start | bytes 196616 | tf_op jit(solution)/shard_map/ppermute | solution.py:30
  88.1 26.3 %all-to-all-start.2 = ((bf16[16,64,256]{2,1,0:T(8,128)(2,1)}), bf16[16,64,256]{2,1,0:T(8,128)(2,1)}, u32[]{:S(2)}, u32[]{:S(2)}) async-start(bf16[16,64,256]{2,1,0:T(8,128)(2,1)} %broadcast_in_dim.14), calls=%async_computation.2 | async-start | bytes 1048576 | tf_op jit(solution)/shard_map/all_to_all | solution.py:21
  95.4 1.6 copy-start.1
  116.2 10.8 %collective-permute-start.2 = (f32[16,32,256]{2,1,0:T(8,128)S(1)}, f32[16,32,256]{2,1,0:T(8,128)S(1)}, u32[]{:S(2)}, u32[]{:S(2)}) collective-permute-start(f32[16,32,256]{2,1,0:T(8,128)S(1)} %dynamic-slice_bitcast_fusion), channel_id=1, source_target_pairs={{0,1},{1,0},{2,3},{3,2},{4,5},{5,4},{6,7},{7,6},{8,9},{9,8},{10,11... | collective-permute-start | bytes 1572872 | tf_op jit(solution)/shard_map/ppermute | solution.py:30
  141.7 63.7 %copy-start.2 = (f32[32,256]{1,0:T(8,128)}, f32[32,256]{1,0:T(8,128)S(1)}, u32[]{:S(2)}) copy-start(f32[32,256]{1,0:T(8,128)S(1)} %multiply_reduce_fusion.1.right_ref) | copy-start | bytes 98308
where the time goes:
time: 217 us; the launch traced here: 215 us
  blocking collectives  121 us (56%)
  starting transfers between devices  39.3 us (18%)
  waiting for transfers between devices  31.5 us (15%)
  Pallas kernels  10 us (5%)
  local copies, waits for them, and re-layouts  7.27 us (3%)
  matrix products  2.85 us (1%)
  other arithmetic  2.26 us (1%)
    all_to_all x5, blocking collectives, exchange(): return lax.all_to_all(blocks, axis, split_axis=0, concat_axis=0, tiled=True)  121 us
    ppermute x3, starting transfers between devices, swap(): return lax.ppermute(block, axis, [(0, 1), (1, 0)])  26.7 us
    all_to_all x2, waiting for transfers between devices, exchange(): return lax.all_to_all(blocks, axis, split_axis=0, concat_axis=0, tiled=True)  25.3 us
    all_to_all x2, starting transfers between devices, exchange(): return lax.all_to_all(blocks, axis, split_axis=0, concat_axis=0, tiled=True)  12.6 us
    pallas_call x1, Pallas kernels, cholesky_qr(): pl.pallas_call(functools.partial(cholesky_qr_kernel, scale), out_shape=(j...  10 us
    ppermute x3, waiting for transfers between devices, swap(): return lax.ppermute(block, axis, [(0, 1), (1, 0)])  6.19 us
  transfers between devices with their start and end apart: 5, of which 5 were waited for; matrix products, arithmetic and copies ran while one was open for 2% of the time, Pallas kernels for 0%

commit v1 on v0

--- a/solution.py
+++ b/solution.py
@@ -68,6 +68,7 @@
 SUB = 8
 LANES = 128
 PANEL = 64
+GROUP = 16
 
 
 def eliminate(panel, first):
@@ -80,27 +81,29 @@
         return jnp.concatenate([a] * (width // LANES), axis=1)
 
     done = []
-    for t in range(tiles):
-        at = first + t * SUB
-        pivots = jnp.zeros((SUB, LANES), jnp.float32)
+    for start in range(0, tiles, GROUP // SUB):
+        at = first + start * SUB
+        pivots = [jnp.zeros((SUB, LANES), jnp.float32) for _ in range(GROUP // SUB)]
         columns = {
-            v: [jnp.broadcast_to(rows[v][:, at + k : at + k + 1], (SUB, LANES)) for k in range(SUB)]
-            for v in range(t, tiles)
+            v: [jnp.broadcast_to(rows[v][:, at + k : at + k + 1], (SUB, LANES)) for k in range(GROUP)]
+            for v in range(start, tiles)
         }
-        for k in range(SUB):
-            pivot = jnp.broadcast_to(columns[t][k][k : k + 1], (SUB, LANES))
+        for k in range(GROUP):
+            i, r = divmod(k, SUB)
+            t = start + i
+            pivot = jnp.broadcast_to(columns[t][k][r : r + 1], (SUB, LANES))
             inverse = 1.0 / pivot
-            pivots = jnp.where(sub == k, pivot, pivots)
-            row = jnp.broadcast_to(rows[t][k : k + 1], (SUB, width))
-            heads = [jnp.broadcast_to(columns[t][l][k : k + 1], (SUB, LANES)) for l in range(k + 1, SUB)]
+            pivots[i] = jnp.where(sub == r, pivot, pivots[i])
+            row = jnp.broadcast_to(rows[t][r : r + 1], (SUB, width))
+            heads = [jnp.broadcast_to(columns[t][l][r : r + 1], (SUB, LANES)) for l in range(k + 1, GROUP)]
             for v in range(t, tiles):
                 times = columns[v][k] * inverse
                 if v == t:
-                    times = jnp.where(sub > k, times, 0.0)
+                    times = jnp.where(sub > r, times, 0.0)
                 rows[v] = rows[v] - wide(times) * row
-                for l in range(k + 1, SUB):
+                for l in range(k + 1, GROUP):
                     columns[v][l] = columns[v][l] - times * heads[l - k - 1]
-        done.append(rows[t] * wide(lax.rsqrt(pivots)))
+        done += [rows[start + i] * wide(lax.rsqrt(pivots[i])) for i in range(GROUP // SUB)]
     return jnp.concatenate(done, axis=0)
 
 
@@ -171,7 +174,8 @@
     gram_part = jnp.dot(
         mine.T, mine, precision=lax.Precision.HIGHEST, preferred_element_type=jnp.float32
     )
-    gram_rows = jnp.sum(spread(scatter_sum(gram_part, PLANE), (Z, CORE)), axis=0)
+    gram_rows = jnp.sum(spread(scatter_sum(gram_part, PLANE), Z), axis=0)
+    gram_rows = gram_rows + swap(gram_rows, CORE)
     gram = spread(gram_rows, PLANE).reshape(k, k)
     scale = math.sqrt(cols * lax.axis_size(ROW))
     factor, basis = cholesky_qr(gram, mine, scale)

time: 217 us -> 210 us (0.968)
  blocking collectives: 121 us -> 108 us
  starting transfers between devices: 39.3 us -> 46.5 us
    all_to_all x5, blocking collectives: 121 us -> 108 us  [exchange(): return lax.all_to_all(blocks, axis, split_axis=0, concat_axis=0, tiled=True)]
    ppermute x3 -> x4, starting transfers between devices: 26.7 us -> 33.8 us  [swap(): return lax.ppermute(block, axis, [(0, 1), (1, 0)])]
    ppermute x3 -> x4, waiting for transfers between devices: 6.19 us -> 7 us  [swap(): return lax.ppermute(block, axis, [(0, 1), (1, 0)])]
  transfers between devices with their start and end apart: 5 -> 6, of which waited for: 5 -> 6; matrix products, arithmetic and copies ran while one was open for 2% -> 2% of each run, Pallas kernels for 0% -> 0%
where the time goes in v1:
time: 210 us; the launch traced here: 209 us
  blocking collectives  108 us (51%)
  starting transfers between devices  46.5 us (22%)
  waiting for transfers between devices  32.3 us (15%)
  Pallas kernels  9.2 us (4%)
  local copies, waits for them, and re-layouts  7.27 us (3%)
  matrix products  2.85 us (1%)
  other arithmetic  2.24 us (1%)
    all_to_all x5, blocking collectives, exchange(): return lax.all_to_all(blocks, axis, split_axis=0, concat_axis=0, tiled=True)  108 us
    ppermute x4, starting transfers between devices, swap(): return lax.ppermute(block, axis, [(0, 1), (1, 0)])  33.8 us
    all_to_all x2, waiting for transfers between devices, exchange(): return lax.all_to_all(blocks, axis, split_axis=0, concat_axis=0, tiled=True)  25.3 us
    all_to_all x2, starting transfers between devices, exchange(): return lax.all_to_all(blocks, axis, split_axis=0, concat_axis=0, tiled=True)  12.6 us
    pallas_call x1, Pallas kernels, cholesky_qr(): pl.pallas_call(functools.partial(cholesky_qr_kernel, scale), out_shape=(j...  9.2 us
    ppermute x4, waiting for transfers between devices, swap(): return lax.ppermute(block, axis, [(0, 1), (1, 0)])  7 us
  transfers between devices with their start and end apart: 6, of which 6 were waited for; matrix products, arithmetic and copies ran while one was open for 2% of the time, Pallas kernels for 0%

profile of v1, /device:TPU:1, one launch (start us, length us, event | category | flops | bytes accessed | tf_op | source)
XLA Modules:
  0.0 209.0 jit_solution(16481998348481159901)
XLA Ops:
  0.6 0.0 copy-start
  0.6 1.6 broadcast_in_dim.12
  2.2 8.0 %all-to-all-start = ((bf16[16,8,1024]{2,1,0:T(8,128)(2,1)}), bf16[16,8,1024]{2,1,0:T(8,128)(2,1)S(1)}, u32[]{:S(2)}, u32[]{:S(2)}) async-start(bf16[16,8,1024]{2,1,0:T(8,128)(2,1)} %broadcast_in_dim.12), calls=%async_computation | async-start | bytes 524288 | tf_op jit(solution)/shard_map/all_to_all | solution.py:21
  10.2 0.7 convert_element_type.44
  10.9 8.1 %all-to-all-done = bf16[16,8,1024]{2,1,0:T(8,128)(2,1)S(1)} async-done(((bf16[16,8,1024]{2,1,0:T(8,128)(2,1)}), bf16[16,8,1024]{2,1,0:T(8,128)(2,1)S(1)}, u32[]{:S(2)}, u32[]{:S(2)}) %all-to-all-start) | async-done | bytes 262176 | tf_op jit(solution)/shard_map/all_to_all | solution.py:21
  19.1 12.7 %collective-permute-start = (bf16[16,8,1024]{2,1,0:T(8,128)(2,1)S(1)}, bf16[16,8,1024]{2,1,0:T(8,128)(2,1)S(1)}, u32[]{:S(2)}, u32[]{:S(2)}) collective-permute-start(bf16[16,8,1024]{2,1,0:T(8,128)(2,1)S(1)} %all-to-all-done), channel_id=1, source_target_pairs={{0,1},{1,0},{2,3},{3,2},{4,5},{5,4},{6,7},{7,6},{8,9},{9,8},{10,11... | collective-permute-start | bytes 786440 | tf_op jit(solution)/shard_map/ppermute | solution.py:30
  31.8 0.3 mul.83
  32.1 0.0 copy-done
  32.1 0.3 bitcast_multiply_fusion
  32.4 0.5 collective-permute-done
  33.0 0.1 pad_maximum_fusion
  33.0 0.8 abs_reduce_fusion
  33.8 0.2 round-nearest-even_convert_fusion
  34.0 0.0 copy-start.3
  34.1 44.0 %all_to_all.35 = s16[16,72,256]{2,1,0:T(8,128)(2,1)S(1)} all-to-all(s16[16,72,256]{2,1,0:T(8,128)(2,1)S(1)} %pad_add_fusion), channel_id=1, replica_groups=mesh['z'=16,'y_hi'=2,'y_lo'=4,'x'=4,'core'=2] {'z'}, dimensions={0} | all-to-all | bytes 1179648 | tf_op jit(solution)/shard_map/all_to_all | solution.py:21
  78.1 0.2 multiply_reduce_fusion
  78.3 4.7 %collective-permute-start.1 = (f32[64,256]{1,0:T(8,128)S(1)}, f32[64,256]{1,0:T(8,128)S(1)}, u32[]{:S(2)}, u32[]{:S(2)}) collective-permute-start(f32[64,256]{1,0:T(8,128)S(1)} %multiply_reduce_fusion), channel_id=1, source_target_pairs={{0,32},{32,0},{1,33},{33,1},{2,34},{34,2},{3,35},{35,3},{4,36},{36... | collective-permute-start | bytes 196616 | tf_op jit(solution)/shard_map/ppermute | solution.py:30
  83.0 4.2 %collective-permute-done.1 = f32[64,256]{1,0:T(8,128)S(1)} collective-permute-done((f32[64,256]{1,0:T(8,128)S(1)}, f32[64,256]{1,0:T(8,128)S(1)}, u32[]{:S(2)}, u32[]{:S(2)}) %collective-permute-start.1) | collective-permute-done | bytes 65568 | tf_op jit(solution)/shard_map/ppermute | solution.py:30
  87.2 0.9 broadcast_in_dim.14
  88.1 4.6 %all-to-all-start.2 = ((bf16[16,64,256]{2,1,0:T(8,128)(2,1)}), bf16[16,64,256]{2,1,0:T(8,128)(2,1)}, u32[]{:S(2)}, u32[]{:S(2)}) async-start(bf16[16,64,256]{2,1,0:T(8,128)(2,1)} %broadcast_in_dim.14), calls=%async_computation.2 | async-start | bytes 1048576 | tf_op jit(solution)/shard_map/all_to_all | solution.py:21
  92.7 0.0 copy-done.3
  92.7 0.1 copy.23
  92.8 2.6 %copy.24 = bf16[1024,1024]{0,1:T(8,128)(2,1)} copy(bf16[1024,1024]{1,0:T(8,128)(2,1)S(1)} %copy-done) | data formatting | bytes 4194304 | tf_op jit(solution)/shard_map/optimization_barrier | solution.py:161
  95.4 0.0 copy-start.1
  95.4 0.3 mul.80
  95.7 1.2 copy-done.1
  97.0 0.3 bitcast_multiply_fusion.1
  97.3 17.1 %all-to-all-done.2 = bf16[16,64,256]{2,1,0:T(8,128)(2,1)} async-done(((bf16[16,64,256]{2,1,0:T(8,128)(2,1)}), bf16[16,64,256]{2,1,0:T(8,128)(2,1)}, u32[]{:S(2)}, u32[]{:S(2)}) %all-to-all-start.2) | async-done | bytes 524320 | tf_op jit(solution)/shard_map/all_to_all | solution.py:21
  114.4 1.8 fusion.5
  116.2 9.2 %collective-permute-start.2 = (f32[16,32,256]{2,1,0:T(8,128)S(1)}, f32[16,32,256]{2,1,0:T(8,128)S(1)}, u32[]{:S(2)}, u32[]{:S(2)}) collective-permute-start(f32[16,32,256]{2,1,0:T(8,128)S(1)} %dynamic-slice_bitcast_fusion), channel_id=1, source_target_pairs={{0,1},{1,0},{2,3},{3,2},{4,5},{5,4},{6,7},{7,6},{8,9},{9,8},{10,11... | collective-permute-start | bytes 1572872 | tf_op jit(solution)/shard_map/ppermute | solution.py:30
  125.5 1.5 collective-permute-done.2
  127.0 0.1 abs_reduce_fusion.1
  127.1 0.1 round-nearest-even_convert_fusion.1
  127.3 14.2 %all_to_all.36 = s16[16,40,256]{2,1,0:T(8,128)(2,1)S(1)} all-to-all(s16[16,40,256]{2,1,0:T(8,128)(2,1)S(1)} %pad_add_fusion.1), channel_id=1, replica_groups=mesh['z'=16,'y_hi'=2,'y_lo'=4,'x'=4,'core'=2] {'y_lo','x'}, dimensions={0} | all-to-all | bytes 655360 | tf_op jit(solution)/shard_map/all_to_all | solution.py:21
  141.5 0.1 multiply_reduce_fusion.1.right_ref
  141.7 0.0 copy-start.2
  141.7 0.1 copy.28
  141.8 0.3 fusion
  142.1 15.5 %all_to_all.37 = f32[32,8,256]{2,1,0:T(8,128)S(1)} all-to-all(f32[32,8,256]{2,1,0:T(8,128)S(1)} %fusion), channel_id=1, replica_groups=mesh['z'=16,'y_hi'=2,'y_lo'=4,'x'=4,'core'=2] {'y_hi','y_lo','x'}, dimensions={0} | all-to-all | bytes 524288 | tf_op jit(solution)/shard_map/all_to_all | solution.py:21
  157.6 18.6 %all_to_all.38 = f32[16,8,256]{2,1,0:T(8,128)S(1)} all-to-all(f32[16,8,256]{2,1,0:T(8,128)S(1)} %broadcast_in_dim.16), channel_id=1, replica_groups=mesh['z'=16,'y_hi'=2,'y_lo'=4,'x'=4,'core'=2] {'z'}, dimensions={0} | all-to-all | bytes 262144 | tf_op jit(solution)/shard_map/all_to_all | solution.py:21
  176.2 7.1 %collective-permute-start.3 = (f32[8,256]{1,0:T(8,128)S(1)}, f32[8,256]{1,0:T(8,128)S(1)}, u32[]{:S(2)}, u32[]{:S(2)}) collective-permute-start(f32[8,256]{1,0:T(8,128)S(1)} %reduce_sum.39), channel_id=1, source_target_pairs={{0,1},{1,0},{2,3},{3,2},{4,5},{5,4},{6,7},{7,6},{8,9},{9,8},{10,11... | collective-permute-start | bytes 24584 | tf_op jit(solution)/shard_map/ppermute | solution.py:30
  183.4 0.8 collective-permute-done.3
  184.2 15.6 %all_to_all.39 = f32[32,8,256]{2,1,0:T(8,128)} all-to-all(f32[32,8,256]{2,1,0:T(8,128)S(1)} %broadcast_in_dim.17), channel_id=1, replica_groups=mesh['z'=16,'y_hi'=2,'y_lo'=4,'x'=4,'core'=2] {'y_hi','y_lo','x'}, dimensions={0} | all-to-all | bytes 524288 | tf_op jit(solution)/shard_map/all_to_all | solution.py:21
  199.8 0.0 copy-done.2
  199.8 9.2 %cholesky_qr.1 = (f32[256,256]{1,0:T(8,128)}, f32[32,256]{1,0:T(8,128)}) custom-call(f32[256,256]{1,0:T(8,128)} %bitcast.57, f32[32,256]{1,0:T(8,128)} %copy-done.2), custom_call_target="tpu_custom_call" | custom-call | tf_op jit(solution)/shard_map/cholesky_qr/pallas_call | solution.py:140
  (19 shorter events, 0.4 us)
Async XLA Ops:
  0.6 31.5 %copy-start = (bf16[1024,1024]{1,0:T(8,128)(2,1)S(1)}, bf16[1024,1024]{1,0:T(8,128)(2,1)}, u32[]{:S(2)}) copy-start(bf16[1024,1024]{1,0:T(8,128)(2,1)} %param.3) | copy-start | bytes 6291460
  2.2 16.8 %all-to-all-start = ((bf16[16,8,1024]{2,1,0:T(8,128)(2,1)}), bf16[16,8,1024]{2,1,0:T(8,128)(2,1)S(1)}, u32[]{:S(2)}, u32[]{:S(2)}) async-start(bf16[16,8,1024]{2,1,0:T(8,128)(2,1)} %broadcast_in_dim.12), calls=%async_computation | async-start | bytes 524288 | tf_op jit(solution)/shard_map/all_to_all | solution.py:21
  19.1 13.9 %collective-permute-start = (bf16[16,8,1024]{2,1,0:T(8,128)(2,1)S(1)}, bf16[16,8,1024]{2,1,0:T(8,128)(2,1)S(1)}, u32[]{:S(2)}, u32[]{:S(2)}) collective-permute-start(bf16[16,8,1024]{2,1,0:T(8,128)(2,1)S(1)} %all-to-all-done), channel_id=1, source_target_pairs={{0,1},{1,0},{2,3},{3,2},{4,5},{5,4},{6,7},{7,6},{8,9},{9,8},{10,11... | collective-permute-start | bytes 786440 | tf_op jit(solution)/shard_map/ppermute | solution.py:30
  34.0 58.7 %copy-start.3 = (s32[8,8]{1,0:T(8,128)S(1)}, s32[8,8]{1,0:T(8,128)}, u32[]{:S(2)}) copy-start(s32[8,8]{1,0:T(8,128)} %param.4) | copy-start | bytes 772
  78.3 8.9 %collective-permute-start.1 = (f32[64,256]{1,0:T(8,128)S(1)}, f32[64,256]{1,0:T(8,128)S(1)}, u32[]{:S(2)}, u32[]{:S(2)}) collective-permute-start(f32[64,256]{1,0:T(8,128)S(1)} %multiply_reduce_fusion), channel_id=1, source_target_pairs={{0,32},{32,0},{1,33},{33,1},{2,34},{34,2},{3,35},{35,3},{4,36},{36... | collective-permute-start | bytes 196616 | tf_op jit(solution)/shard_map/ppermute | solution.py:30
  88.1 26.3 %all-to-all-start.2 = ((bf16[16,64,256]{2,1,0:T(8,128)(2,1)}), bf16[16,64,256]{2,1,0:T(8,128)(2,1)}, u32[]{:S(2)}, u32[]{:S(2)}) async-start(bf16[16,64,256]{2,1,0:T(8,128)(2,1)} %broadcast_in_dim.14), calls=%async_computation.2 | async-start | bytes 1048576 | tf_op jit(solution)/shard_map/all_to_all | solution.py:21
  95.4 1.6 copy-start.1
  116.2 10.8 %collective-permute-start.2 = (f32[16,32,256]{2,1,0:T(8,128)S(1)}, f32[16,32,256]{2,1,0:T(8,128)S(1)}, u32[]{:S(2)}, u32[]{:S(2)}) collective-permute-start(f32[16,32,256]{2,1,0:T(8,128)S(1)} %dynamic-slice_bitcast_fusion), channel_id=1, source_target_pairs={{0,1},{1,0},{2,3},{3,2},{4,5},{5,4},{6,7},{7,6},{8,9},{9,8},{10,11... | collective-permute-start | bytes 1572872 | tf_op jit(solution)/shard_map/ppermute | solution.py:30
  141.7 58.1 %copy-start.2 = (f32[32,256]{1,0:T(8,128)}, f32[32,256]{1,0:T(8,128)S(1)}, u32[]{:S(2)}) copy-start(f32[32,256]{1,0:T(8,128)S(1)} %multiply_reduce_fusion.1.right_ref) | copy-start | bytes 98308
  176.2 8.0 %collective-permute-start.3 = (f32[8,256]{1,0:T(8,128)S(1)}, f32[8,256]{1,0:T(8,128)S(1)}, u32[]{:S(2)}, u32[]{:S(2)}) collective-permute-start(f32[8,256]{1,0:T(8,128)S(1)} %reduce_sum.39), channel_id=1, source_target_pairs={{0,1},{1,0},{2,3},{3,2},{4,5},{5,4},{6,7},{7,6},{8,9},{9,8},{10,11... | collective-permute-start | bytes 24584 | tf_op jit(solution)/shard_map/ppermute | solution.py:30
